TPU v7x, 32 devices: a whole 2x2x4 slice. The times are simulated.
32 devices in a mesh: sub: 8 (over z, y), grp: 4 (over x, core).
Axes of the slice: x: 2, y: 2, z: 4, core: 2. Of those that a mesh axis runs over, the one named last changes fastest.
Arguments:
- right_side: float32 [512, 8192], P('grp', 'sub'), may hold values from -6 to 6
- operator_block: bfloat16 [8192, 1024], P('sub'), may hold values from -0.1875 to 0.1875
- operator_diag: float32 [8192], P('sub'), may hold values from 2 to 4
- solve_block: bfloat16 [8192, 1024], P('sub'), may hold values from -0.1875 to 0.1875
- solve_diag: float32 [8192], P('sub'), may hold values from 0.5 to 1.5
- upper_rows: int32 [8, 128], P('sub'), may hold values from 0 to 1023, as said below
- lower_rows: int32 [8, 128], P('sub'), may hold values from 0 to 1023, as said below
- couple_up: bfloat16 [1024, 128], P('sub'), may hold values from -0.5 to 0.5
- couple_down: bfloat16 [1024, 128], P('sub'), may hold values from -0.5 to 0.5
- coarse_basis: bfloat16 [64, 8192], P(None, 'sub'), may hold values from -0.75 to 0.75
- coarse_inverse: bfloat16 [512, 512], P(('sub', 'grp')), may hold values from -0.046875 to 0.046875
Outputs:
- solution: float32 [512, 8192], P('grp', 'sub')
Inputs may be any that keep to these rules, and one draw needn't show every extreme that they name: `upper_rows`: local row numbers within a subdomain of 1024 unknowns; the 128 entries of one subdomain are distinct, and none of them appears in lower_rows of the same subdomain. `lower_rows`: local row numbers within a subdomain of 1024 unknowns; the 128 entries of one subdomain are distinct, and none of them appears in upper_rows of the same subdomain.
All inputs are finite; a program needn't handle non-finite values.
Results may differ from a plain program's by a relative error of at most 0.0042.
Values may be sent and summed in bfloat16 or wider, within the bound.
A program may use at most 64 MiB of HBM per device.

v0:
```python
import jax
import jax.numpy as jnp
from jax import lax
from jax.sharding import PartitionSpec as P

ITERS = 3
EPS = 1e-06


def extended(block, sides, width):
    for axis, dim in sides:
        count = lax.axis_size(axis)
        forward = [(i, i + 1) for i in range(count - 1)]
        forward.append((count - 1, 0))
        backward = [(target, source) for source, target in forward]
        low = lax.ppermute(
            lax.slice_in_dim(block, block.shape[dim] - width, None, axis=dim), axis, forward
        )
        high = lax.ppermute(lax.slice_in_dim(block, 0, width, axis=dim), axis, backward)
        block = jnp.concatenate([low, block, high], axis=dim)
    return block


def contract_last(left, right):
    return lax.dot_general(
        left, right, (((1,), (1,)), ((), ())), preferred_element_type=jnp.float32
    )


def apply_operator(
    vector, operator_block, operator_diag, upper_list, lower_list, couple_up, couple_down
):
    vector_b = vector.astype(jnp.bfloat16)
    product = contract_last(vector_b, operator_block)
    face_count = upper_list.shape[0]
    upper_face = jnp.take(vector_b, upper_list, axis=1)
    lower_face = jnp.take(vector_b, lower_list, axis=1)
    two_faces = jnp.concatenate([lower_face, upper_face], axis=1)
    padded = extended(two_faces, (("sub", 1),), face_count)
    from_below = padded[:, :face_count]
    from_above = padded[:, 3 * face_count :]
    into_upper = jnp.dot(from_above, couple_up, preferred_element_type=jnp.float32)
    into_lower = jnp.dot(from_below, couple_down, preferred_element_type=jnp.float32)
    result = operator_diag[None, :] * vector + product
    result = result.at[:, upper_list].add(into_upper)
    result = result.at[:, lower_list].add(into_lower)
    return result


def apply_solve(vector, solve_block, solve_diag, coarse_basis, coarse_inverse):
    vector_b = vector.astype(jnp.bfloat16)
    local_term = contract_last(vector_b, solve_block)
    partial_res = contract_last(coarse_basis, vector_b).astype(jnp.bfloat16)
    widened = lax.all_gather(partial_res, "grp", axis=1, tiled=True)
    solved_part = jnp.dot(
        coarse_inverse,
        lax.all_gather(widened, "sub", axis=0, tiled=True),
        preferred_element_type=jnp.float32,
    ).astype(jnp.bfloat16)
    solved = lax.all_to_all(solved_part, "grp", split_axis=1, concat_axis=0, tiled=True)
    coarse_term = lax.dot_general(
        solved, coarse_basis, (((0,), (0,)), ((), ())), preferred_element_type=jnp.float32
    )
    return solve_diag[None, :] * vector + local_term + coarse_term


def norm_of(vector):
    squares = jnp.sum(vector * vector, axis=1)
    return jnp.sqrt(lax.psum(squares, "sub") + EPS)


def least_squares(initial_norm, columns):
    extent = len(columns)
    rotations = []
    target = [initial_norm] + [jnp.zeros_like(initial_norm) for _ in range(extent)]
    triangle = []
    for j in range(extent):
        column = list(columns[j])
        for i in range(j):
            cosine, sine_value = rotations[i]
            leading = cosine * column[i] + sine_value * column[i + 1]
            column[i + 1] = -sine_value * column[i] + cosine * column[i + 1]
            column[i] = leading
        radius = jnp.sqrt(column[j] * column[j] + column[j + 1] * column[j + 1])
        cosine = column[j] / radius
        sine_value = column[j + 1] / radius
        column[j] = radius
        rotations.append((cosine, sine_value))
        target[j + 1] = -sine_value * target[j]
        target[j] = cosine * target[j]
        triangle.append(column[: j + 1])
    coeffs = [None] * extent
    for j in reversed(range(extent)):
        partial_sum = target[j]
        for k in range(j + 1, extent):
            partial_sum = partial_sum - triangle[k][j] * coeffs[k]
        coeffs[j] = partial_sum / triangle[j][j]
    return coeffs


def on_device(
    right_side,
    operator_block,
    operator_diag,
    solve_block,
    solve_diag,
    upper_rows,
    lower_rows,
    couple_up,
    couple_down,
    coarse_basis,
    coarse_inverse,
):
    upper_list = upper_rows.reshape(-1)
    lower_list = lower_rows.reshape(-1)

    def precond(vector):
        return apply_solve(vector, solve_block, solve_diag, coarse_basis, coarse_inverse)

    residual = precond(right_side)
    initial_norm = norm_of(residual)
    krylov = [residual / initial_norm[:, None]]
    columns = []
    for iteration in range(ITERS):
        candidate = precond(
            apply_operator(
                krylov[iteration],
                operator_block,
                operator_diag,
                upper_list,
                lower_list,
                couple_up,
                couple_down,
            )
        )
        heights = []
        for i in range(iteration + 1):
            height_i = lax.psum(jnp.sum(candidate * krylov[i], axis=1), "sub")
            heights.append(height_i)
            candidate = candidate - height_i[:, None] * krylov[i]
        height = norm_of(candidate)
        heights.append(height)
        krylov.append(candidate / height[:, None])
        columns.append(heights)
    coeffs = least_squares(initial_norm, columns)
    solution = coeffs[0][:, None] * krylov[0]
    for j in range(1, ITERS):
        solution = solution + coeffs[j][:, None] * krylov[j]
    return solution


def solution(mesh):
    return jax.shard_map(
        on_device,
        mesh=mesh,
        in_specs=(
            P("grp", "sub"),
            P("sub", None),
            P("sub"),
            P("sub", None),
            P("sub"),
            P("sub", None),
            P("sub", None),
            P("sub", None),
            P("sub", None),
            P(None, "sub"),
            P(("sub", "grp"), None),
        ),
        out_specs=P("grp", "sub"),
        check_vma=False,
    )
```

profile of v0, /device:TPU:0, one launch (start us, length us, event | category | flops | bytes accessed | tf_op | source)
XLA Modules:
  0.0 463.0 jit_solution(12258683345657579884)
XLA Ops:
  1.5 6.2 %all_gather.24 = bf16[64,512]{1,0:T(8,128)(2,1)S(1)} all-gather(bf16[64,128]{1,0:T(8,128)(2,1)S(1)} %convolution_convert_fusion.7), channel_id=1, replica_groups=mesh['sub'=8,'grp'=4] {'grp'}, dimensions={1}, use_global_device_ids=true | all-gather | bytes 81920 | tf_op jit(solution)/shard_map/all_gather | solution.py:54
  7.7 32.6 %all_gather.25 = bf16[512,512]{1,0:T(8,128)(2,1)S(1)} all-gather(bf16[64,512]{1,0:T(8,128)(2,1)S(1)} %all_gather.24), channel_id=1, replica_groups=mesh['sub'=8,'grp'=4] {'sub'}, dimensions={0}, use_global_device_ids=true | all-gather | bytes 589824 | tf_op jit(solution)/shard_map/all_gather | solution.py:57
  41.7 3.2 all-to-all-start
  53.7 21.2 %psum.70 = f32[128]{0:T(128)S(1)} all-reduce(f32[128]{0:T(128)S(1)} %get-tuple-element.18), channel_id=1, replica_groups=mesh['sub'=8,'grp'=4] {'sub'}, use_global_device_ids=true, to_apply=%region_1.0 | all-reduce | flops 128 | bytes 1024 | tf_op jit(solution)/shard_map/psum | solution.py:69
  77.0 4.7 %collective-permute-start = (bf16[128,128]{0,1:T(8,128)(2,1)S(1)}, bf16[128,128]{0,1:T(8,128)(2,1)S(1)}, u32[]{:S(2)}, u32[]{:S(2)}) collective-permute-start(bf16[128,128]{0,1:T(8,128)(2,1)S(1)} %select_bitcast_fusion.5), channel_id=1, source_target_pairs={{4,0},{8,4},{12,8},{16,12},{20,16},{24,20},{28,24},{0,28},{5,1},{9... | collective-permute-start | bytes 98312 | tf_op jit(solution)/shard_map/ppermute | solution.py:19
  91.2 5.3 %all_gather.26 = bf16[64,512]{1,0:T(8,128)(2,1)S(1)} all-gather(bf16[64,128]{1,0:T(8,128)(2,1)S(1)} %fusion.1), channel_id=1, replica_groups=mesh['sub'=8,'grp'=4] {'grp'}, dimensions={1}, use_global_device_ids=true | all-gather | bytes 81920 | tf_op jit(solution)/shard_map/all_gather | solution.py:54
  96.4 31.3 %all_gather.27 = bf16[512,512]{1,0:T(8,128)(2,1)S(1)} all-gather(bf16[64,512]{1,0:T(8,128)(2,1)S(1)} %all_gather.26), channel_id=1, replica_groups=mesh['sub'=8,'grp'=4] {'sub'}, dimensions={0}, use_global_device_ids=true | all-gather | bytes 589824 | tf_op jit(solution)/shard_map/all_gather | solution.py:57
  128.5 3.2 all-to-all-start.1
  137.0 19.2 %psum.71 = f32[128]{0:T(128)S(1)} all-reduce(f32[128]{0:T(128)S(1)} %get-tuple-element.20), channel_id=1, replica_groups=mesh['sub'=8,'grp'=4] {'sub'}, use_global_device_ids=true, to_apply=%region_5.7 | all-reduce | flops 128 | bytes 1024 | tf_op jit(solution)/shard_map/psum | solution.py:138
  156.4 17.1 %psum.72 = f32[128]{0:T(128)S(1)} all-reduce(f32[128]{0:T(128)S(1)} %multiply_reduce_fusion.7), channel_id=1, replica_groups=mesh['sub'=8,'grp'=4] {'sub'}, use_global_device_ids=true, to_apply=%region_7.9 | all-reduce | flops 128 | bytes 1024 | tf_op jit(solution)/shard_map/psum | solution.py:69
  202.1 5.3 %all_gather.28 = bf16[64,512]{1,0:T(8,128)(2,1)S(1)} all-gather(bf16[64,128]{1,0:T(8,128)(2,1)S(1)} %fusion.3), channel_id=1, replica_groups=mesh['sub'=8,'grp'=4] {'grp'}, dimensions={1}, use_global_device_ids=true | all-gather | bytes 81920 | tf_op jit(solution)/shard_map/all_gather | solution.py:54
  207.3 31.5 %all_gather.29 = bf16[512,512]{1,0:T(8,128)(2,1)S(1)} all-gather(bf16[64,512]{1,0:T(8,128)(2,1)S(1)} %all_gather.28), channel_id=1, replica_groups=mesh['sub'=8,'grp'=4] {'sub'}, dimensions={0}, use_global_device_ids=true | all-gather | bytes 589824 | tf_op jit(solution)/shard_map/all_gather | solution.py:57
  248.8 18.0 %psum.73 = f32[128]{0:T(128)S(1)} all-reduce(f32[128]{0:T(128)S(1)} %get-tuple-element.22), channel_id=1, replica_groups=mesh['sub'=8,'grp'=4] {'sub'}, use_global_device_ids=true, to_apply=%region_11.13 | all-reduce | flops 128 | bytes 1024 | tf_op jit(solution)/shard_map/psum | solution.py:138
  268.1 18.3 %psum.74 = f32[128]{0:T(128)S(1)} all-reduce(f32[128]{0:T(128)S(1)} %multiply_reduce_fusion.5), channel_id=1, replica_groups=mesh['sub'=8,'grp'=4] {'sub'}, use_global_device_ids=true, to_apply=%region_13.15 | all-reduce | flops 128 | bytes 1024 | tf_op jit(solution)/shard_map/psum | solution.py:138
  288.4 18.2 %psum.75 = f32[128]{0:T(128)S(1)} all-reduce(f32[128]{0:T(128)S(1)} %get-tuple-element.14), channel_id=1, replica_groups=mesh['sub'=8,'grp'=4] {'sub'}, use_global_device_ids=true, to_apply=%region_15.17 | all-reduce | flops 128 | bytes 1024 | tf_op jit(solution)/shard_map/psum | solution.py:69
  313.0 3.5 convolution_add_fusion.5
  317.9 3.6 collective-permute-start.4
  334.5 5.3 %all_gather.30 = bf16[64,512]{1,0:T(8,128)(2,1)S(1)} all-gather(bf16[64,128]{1,0:T(8,128)(2,1)S(1)} %fusion.5), channel_id=1, replica_groups=mesh['sub'=8,'grp'=4] {'grp'}, dimensions={1}, use_global_device_ids=true | all-gather | bytes 81920 | tf_op jit(solution)/shard_map/all_gather | solution.py:54
  339.7 31.5 %all_gather.31 = bf16[512,512]{1,0:T(8,128)(2,1)S(1)} all-gather(bf16[64,512]{1,0:T(8,128)(2,1)S(1)} %all_gather.30), channel_id=1, replica_groups=mesh['sub'=8,'grp'=4] {'sub'}, dimensions={0}, use_global_device_ids=true | all-gather | bytes 589824 | tf_op jit(solution)/shard_map/all_gather | solution.py:57
  372.0 3.2 all-to-all-start.3
  381.1 21.2 %psum.76 = f32[128]{0:T(128)S(1)} all-reduce(f32[128]{0:T(128)S(1)} %get-tuple-element.24), channel_id=1, replica_groups=mesh['sub'=8,'grp'=4] {'sub'}, use_global_device_ids=true, to_apply=%region_19.21 | all-reduce | flops 128 | bytes 1024 | tf_op jit(solution)/shard_map/psum | solution.py:138
  403.7 17.1 %psum.77 = f32[128]{0:T(128)S(1)} all-reduce(f32[128]{0:T(128)S(1)} %multiply_reduce_fusion.2), channel_id=1, replica_groups=mesh['sub'=8,'grp'=4] {'sub'}, use_global_device_ids=true, to_apply=%region_21.23 | all-reduce | flops 128 | bytes 1024 | tf_op jit(solution)/shard_map/psum | solution.py:138
  423.1 19.1 %psum.78 = f32[128]{0:T(128)S(1)} all-reduce(f32[128]{0:T(128)S(1)} %get-tuple-element.12), channel_id=1, replica_groups=mesh['sub'=8,'grp'=4] {'sub'}, use_global_device_ids=true, to_apply=%region_23.25 | all-reduce | flops 128 | bytes 1024 | tf_op jit(solution)/shard_map/psum | solution.py:138
  443.6 17.2 %psum.79 = f32[128]{0:T(128)S(1)} all-reduce(f32[128]{0:T(128)S(1)} %multiply_reduce_fusion), channel_id=1, replica_groups=mesh['sub'=8,'grp'=4] {'sub'}, use_global_device_ids=true, to_apply=%region_25.27 | all-reduce | flops 128 | bytes 1024 | tf_op jit(solution)/shard_map/psum | solution.py:69
  (181 shorter events, 105.4 us)
Async XLA Ops:
  0.0 50.0 %copy-start = (bf16[1024,1024]{1,0:T(8,128)(2,1)S(1)}, bf16[1024,1024]{1,0:T(8,128)(2,1)}, u32[]{:S(2)}) copy-start(bf16[1024,1024]{1,0:T(8,128)(2,1)} %param.16) | copy-start | bytes 6291460
  0.0 50.0 %copy-start.2 = (f32[128,1024]{1,0:T(8,128)S(1)}, f32[128,1024]{1,0:T(8,128)}, u32[]{:S(2)}) copy-start(f32[128,1024]{1,0:T(8,128)} %param.13) | copy-start | bytes 1572868
  7.7 44.7 %copy-start.1 = (bf16[64,1024]{1,0:T(8,128)(2,1)S(1)}, bf16[64,1024]{1,0:T(8,128)(2,1)}, u32[]{:S(2)}) copy-start(bf16[64,1024]{1,0:T(8,128)(2,1)} %param.22) | copy-start | bytes 393220
  41.7 10.6 %all-to-all-start = ((bf16[16,4,128]{2,0,1:T(8,128)(2,1)}), bf16[16,4,128]{2,0,1:T(8,128)(2,1)S(1)}, u32[]{:S(2)}, u32[]{:S(2)}) async-start(bf16[16,4,128]{2,0,1:T(8,128)(2,1)} %bitcast.121), calls=%async_computation | async-start | bytes 32768 | tf_op jit(solution)/shard_map/all_to_all | solution.py:60
  76.8 9.4 %collective-permute-start.1 = (bf16[128,128]{0,1:T(8,128)(2,1)S(1)}, bf16[128,128]{0,1:T(8,128)(2,1)S(1)}, u32[]{:S(2)}, u32[]{:S(2)}) collective-permute-start(bf16[128,128]{0,1:T(8,128)(2,1)S(1)} %select_bitcast_fusion.4), channel_id=1, source_target_pairs={{0,4},{4,8},{8,12},{12,16},{16,20},{20,24},{24,28},{28,0},{1,5},{5... | collective-permute-start | bytes 98312 | tf_op jit(solution)/shard_map/ppermute | solution.py:16
  77.0 9.5 %collective-permute-start = (bf16[128,128]{0,1:T(8,128)(2,1)S(1)}, bf16[128,128]{0,1:T(8,128)(2,1)S(1)}, u32[]{:S(2)}, u32[]{:S(2)}) collective-permute-start(bf16[128,128]{0,1:T(8,128)(2,1)S(1)} %select_bitcast_fusion.5), channel_id=1, source_target_pairs={{4,0},{8,4},{12,8},{16,12},{20,16},{24,20},{28,24},{0,28},{5,1},{9... | collective-permute-start | bytes 98312 | tf_op jit(solution)/shard_map/ppermute | solution.py:19
  86.8 40.9 %copy-start.10 = (bf16[16,512]{1,0:T(8,128)(2,1)S(1)}, bf16[16,512]{1,0:T(8,128)(2,1)}, u32[]{:S(2)}) copy-start(bf16[16,512]{1,0:T(8,128)(2,1)} %param.23) | copy-start | bytes 49156
  88.4 43.4 %copy-start.13 = (f32[1024]{0:T(1024)S(1)}, f32[1024]{0:T(1024)}, u32[]{:S(2)}) copy-start(f32[1024]{0:T(1024)} %param.17) | copy-start | bytes 12292
  128.5 7.1 %all-to-all-start.1 = ((bf16[16,4,128]{2,0,1:T(8,128)(2,1)}), bf16[16,4,128]{2,0,1:T(8,128)(2,1)S(1)}, u32[]{:S(2)}, u32[]{:S(2)}) async-start(bf16[16,4,128]{2,0,1:T(8,128)(2,1)} %bitcast.120), calls=%async_computation.1 | async-start | bytes 32768 | tf_op jit(solution)/shard_map/all_to_all | solution.py:60
  137.0 36.6 %copy-start.3 = (f32[128,1024]{1,0:T(8,128)}, f32[128,1024]{1,0:T(8,128)S(1)}, u32[]{:S(2)}) copy-start(f32[128,1024]{1,0:T(8,128)S(1)} %get-tuple-element.21) | copy-start | bytes 1572868
  181.2 10.0 %collective-permute-start.3 = (bf16[128,128]{0,1:T(8,128)(2,1)S(1)}, bf16[128,128]{0,1:T(8,128)(2,1)S(1)}, u32[]{:S(2)}, u32[]{:S(2)}) collective-permute-start(bf16[128,128]{0,1:T(8,128)(2,1)S(1)} %select_bitcast_fusion.2), channel_id=1, source_target_pairs={{0,4},{4,8},{8,12},{12,16},{16,20},{20,24},{24,28},{28,0},{1,5},{5... | collective-permute-start | bytes 98312 | tf_op jit(solution)/shard_map/ppermute | solution.py:16
  183.3 8.3 %collective-permute-start.2 = (bf16[128,128]{0,1:T(8,128)(2,1)S(1)}, bf16[128,128]{0,1:T(8,128)(2,1)}, u32[]{:S(2)}, u32[]{:S(2)}) collective-permute-start(bf16[128,128]{0,1:T(8,128)(2,1)S(1)} %select_bitcast_fusion.3), channel_id=1, source_target_pairs={{4,0},{8,4},{12,8},{16,12},{20,16},{24,20},{28,24},{0,28},{5,1},{9... | collective-permute-start | bytes 98312 | tf_op jit(solution)/shard_map/ppermute | solution.py:19
  195.7 47.2 %copy-start.14 = (f32[1024]{0:T(1024)S(1)}, f32[1024]{0:T(1024)}, u32[]{:S(2)}) copy-start(f32[1024]{0:T(1024)} %param.17) | copy-start | bytes 12292
  239.7 7.1 %all-to-all-start.2 = ((bf16[16,4,128]{2,0,1:T(8,128)(2,1)}), bf16[16,4,128]{2,0,1:T(8,128)(2,1)S(1)}, u32[]{:S(2)}, u32[]{:S(2)}) async-start(bf16[16,4,128]{2,0,1:T(8,128)(2,1)} %bitcast.119), calls=%async_computation.2 | async-start | bytes 32768 | tf_op jit(solution)/shard_map/all_to_all | solution.py:60
  266.8 39.8 %copy-start.26 = (f32[128]{0:T(128)}, f32[128]{0:T(128)S(1)}, u32[]{:S(2)}) copy-start(f32[128]{0:T(128)S(1)} %psum.73) | copy-start | bytes 1540
  316.6 7.0 %collective-permute-start.5 = (bf16[128,128]{0,1:T(8,128)(2,1)S(1)}, bf16[128,128]{0,1:T(8,128)(2,1)S(1)}, u32[]{:S(2)}, u32[]{:S(2)}) collective-permute-start(bf16[128,128]{0,1:T(8,128)(2,1)S(1)} %select_bitcast_fusion), channel_id=1, source_target_pairs={{0,4},{4,8},{8,12},{12,16},{16,20},{20,24},{24,28},{28,0},{1,5},{5... | collective-permute-start | bytes 98312 | tf_op jit(solution)/shard_map/ppermute | solution.py:16
  317.9 6.0 %collective-permute-start.4 = (bf16[128,128]{0,1:T(8,128)(2,1)S(1)}, bf16[128,128]{0,1:T(8,128)(2,1)}, u32[]{:S(2)}, u32[]{:S(2)}) collective-permute-start(bf16[128,128]{0,1:T(8,128)(2,1)S(1)} %select_bitcast_fusion.1), channel_id=1, source_target_pairs={{4,0},{8,4},{12,8},{16,12},{20,16},{24,20},{28,24},{0,28},{5,1},{9... | collective-permute-start | bytes 98312 | tf_op jit(solution)/shard_map/ppermute | solution.py:19
  328.1 47.1 %copy-start.15 = (f32[1024]{0:T(1024)S(1)}, f32[1024]{0:T(1024)}, u32[]{:S(2)}) copy-start(f32[1024]{0:T(1024)} %param.17) | copy-start | bytes 12292
  372.0 7.1 %all-to-all-start.3 = ((bf16[16,4,128]{2,0,1:T(8,128)(2,1)}), bf16[16,4,128]{2,0,1:T(8,128)(2,1)S(1)}, u32[]{:S(2)}, u32[]{:S(2)}) async-start(bf16[16,4,128]{2,0,1:T(8,128)(2,1)} %bitcast.118), calls=%async_computation.3 | async-start | bytes 32768 | tf_op jit(solution)/shard_map/all_to_all | solution.py:60
  378.0 42.8 %copy-start.23 = (f32[128]{0:T(128)S(1)}, f32[128]{0:T(128)}, u32[]{:S(2)}) copy-start(f32[128]{0:T(128)} %copy-done.22) | copy-start | bytes 1540
  403.6 57.2 %copy-start.27 = (f32[128]{0:T(128)S(1)}, f32[128]{0:T(128)}, u32[]{:S(2)}) copy-start(f32[128]{0:T(128)} %copy-done.26) | copy-start | bytes 1540
  403.7 57.2 %copy-start.34 = (f32[128]{0:T(128)S(1)}, f32[128]{0:T(128)}, u32[]{:S(2)}) copy-start(f32[128]{0:T(128)} %copy-done.33) | copy-start | bytes 1540
  403.7 57.2 %copy-start.38 = (f32[128]{0:T(128)S(1)}, f32[128]{0:T(128)}, u32[]{:S(2)}) copy-start(f32[128]{0:T(128)} %copy-done.37) | copy-start | bytes 1540
  403.7 57.2 %copy-start.40 = (f32[128]{0:T(128)S(1)}, f32[128]{0:T(128)}, u32[]{:S(2)}) copy-start(f32[128]{0:T(128)} %copy-done.39) | copy-start | bytes 1540
  (27 other events, 327.7 us)
where the time goes:
time: 465 us; the launch traced here: 463 us
  blocking collectives  335 us (72%)
  other arithmetic  37.1 us (8%)
  matrix products  35.6 us (8%)
  starting transfers between devices  27.4 us (6%)
  local copies, waits for them, and re-layouts  23.7 us (5%)
    all_gather x4, blocking collectives, apply_solve(): lax.all_gather(widened, 'sub', axis=0, tiled=True)  127 us
    psum x6, blocking collectives, on_device(): height_i = lax.psum(jnp.sum(candidate * krylov[i], axis=1), 'sub')  113 us
    psum x4, blocking collectives, norm_of(): return jnp.sqrt(lax.psum(squares, 'sub') + EPS)  73.7 us
    dot_general x11, matrix products, contract_last(): lax.dot_general(left, right, (((1,), (1,)), ((), ())), preferred_element_...  24.7 us
    all_gather x4, blocking collectives, apply_solve(): widened = lax.all_gather(partial_res, 'grp', axis=1, tiled=True)  21.9 us
    all_to_all x4, starting transfers between devices, apply_solve(): lax.all_to_all(solved_part, 'grp', split_axis=1, concat_axis=0, tiled=True)  13 us
    ppermute x3, starting transfers between devices, extended(): lax.ppermute(lax.slice_in_dim(block, 0, width, axis=dim), axis, backward)  11.1 us
  transfers between devices with their start and end apart: 10, of which 3 were waited for; matrix products, arithmetic and copies ran while one was open for 6% of the time, Pallas kernels for 0%

commit v1 on v0

--- a/solution.py
+++ b/solution.py
@@ -5,6 +5,22 @@
 
 ITERS = 3
 EPS = 1e-06
+
+
+def pairwise_exchange(x, axis, split, join):
+    ways, here = (lax.axis_size(axis), lax.axis_index(axis))
+    width = x.shape[split] // ways
+    dims = list(x.shape)
+    dims[split] = width
+    height = dims[join]
+    dims[join] = height * ways
+    full = jnp.zeros(dims, x.dtype)
+    for mask in range(ways):
+        part = lax.dynamic_slice_in_dim(x, (here ^ mask) * width, width, axis=split)
+        if mask:
+            part = lax.ppermute(part, axis, [(d, d ^ mask) for d in range(ways)])
+        full = lax.dynamic_update_slice_in_dim(full, part, (here ^ mask) * height, axis=join)
+    return full
 
 
 def extended(block, sides, width):
@@ -57,7 +73,7 @@
         lax.all_gather(widened, "sub", axis=0, tiled=True),
         preferred_element_type=jnp.float32,
     ).astype(jnp.bfloat16)
-    solved = lax.all_to_all(solved_part, "grp", split_axis=1, concat_axis=0, tiled=True)
+    solved = pairwise_exchange(solved_part, "grp", 1, 0)
     coarse_term = lax.dot_general(
         solved, coarse_basis, (((0,), (0,)), ((), ())), preferred_element_type=jnp.float32
     )

time: 465 us -> 446 us (0.959)
  matrix products: 35.6 us -> 30.1 us
  starting transfers between devices: 27.4 us -> 21.9 us
    all_to_all x4 -> x0, starting transfers between devices: 13 us -> none  [apply_solve(): lax.all_to_all(solved_part, 'grp', split_axis=1, concat_axis=0, tiled=True)]
    ppermute x0 -> x12, starting transfers between devices: none -> 7.48 us  [pairwise_exchange(): part = lax.ppermute(part, axis, [(d, d ^ mask) for d in range(ways)])]
  transfers between devices with their start and end apart: 10 -> 18, of which waited for: 3 -> 0; matrix products, arithmetic and copies ran while one was open for 6% -> 5% of each run, Pallas kernels for 0% -> 0%
where the time goes in v1:
time: 446 us; the launch traced here: 444 us
  blocking collectives  335 us (75%)
  other arithmetic  34.7 us (8%)
  matrix products  30.1 us (7%)
  starting transfers between devices  21.9 us (5%)
  local copies, waits for them, and re-layouts  21.4 us (5%)
    all_gather x4, blocking collectives, apply_solve(): lax.all_gather(widened, 'sub', axis=0, tiled=True)  127 us
    psum x6, blocking collectives, on_device(): height_i = lax.psum(jnp.sum(candidate * krylov[i], axis=1), 'sub')  113 us
    psum x4, blocking collectives, norm_of(): return jnp.sqrt(lax.psum(squares, 'sub') + EPS)  73.8 us
    dot_general x11, matrix products, contract_last(): lax.dot_general(left, right, (((1,), (1,)), ((), ())), preferred_element_...  22.3 us
    all_gather x4, blocking collectives, apply_solve(): widened = lax.all_gather(partial_res, 'grp', axis=1, tiled=True)  21.9 us
    ppermute x3, starting transfers between devices, extended(): lax.ppermute(lax.slice_in_dim(block, 0, width, axis=dim), axis, backward)  11.3 us
  transfers between devices with their start and end apart: 18, of which 0 were waited for; matrix products, arithmetic and copies ran while one was open for 5% of the time, Pallas kernels for 0%

profile of v1, /device:TPU:0, one launch (start us, length us, event | category | flops | bytes accessed | tf_op | source)
XLA Modules:
  0.0 444.2 jit_solution(5425296165806540518)
XLA Ops:
  1.5 6.2 %all_gather.24 = bf16[64,512]{1,0:T(8,128)(2,1)S(1)} all-gather(bf16[64,128]{1,0:T(8,128)(2,1)S(1)} %convolution_convert_fusion.7), channel_id=1, replica_groups=mesh['sub'=8,'grp'=4] {'grp'}, dimensions={1}, use_global_device_ids=true | all-gather | bytes 81920 | tf_op jit(solution)/shard_map/all_gather | solution.py:70
  7.7 32.6 %all_gather.25 = bf16[512,512]{1,0:T(8,128)(2,1)S(1)} all-gather(bf16[64,512]{1,0:T(8,128)(2,1)S(1)} %all_gather.24), channel_id=1, replica_groups=mesh['sub'=8,'grp'=4] {'sub'}, dimensions={0}, use_global_device_ids=true | all-gather | bytes 589824 | tf_op jit(solution)/shard_map/all_gather | solution.py:73
  49.5 21.2 %psum.70 = f32[128]{0:T(128)S(1)} all-reduce(f32[128]{0:T(128)S(1)} %get-tuple-element.30), channel_id=1, replica_groups=mesh['sub'=8,'grp'=4] {'sub'}, use_global_device_ids=true, to_apply=%region_1.0 | all-reduce | flops 128 | bytes 1024 | tf_op jit(solution)/shard_map/psum | solution.py:85
  72.7 4.8 %collective-permute-start.3 = (bf16[128,128]{0,1:T(8,128)(2,1)S(1)}, bf16[128,128]{0,1:T(8,128)(2,1)S(1)}, u32[]{:S(2)}, u32[]{:S(2)}) collective-permute-start(bf16[128,128]{0,1:T(8,128)(2,1)S(1)} %select_bitcast_fusion.5), channel_id=1, source_target_pairs={{4,0},{8,4},{12,8},{16,12},{20,16},{24,20},{28,24},{0,28},{5,1},{9... | collective-permute-start | bytes 98312 | tf_op jit(solution)/shard_map/ppermute | solution.py:35
  77.4 3.2 multiply_add_fusion.2
  86.9 5.3 %all_gather.26 = bf16[64,512]{1,0:T(8,128)(2,1)S(1)} all-gather(bf16[64,128]{1,0:T(8,128)(2,1)S(1)} %fusion), channel_id=1, replica_groups=mesh['sub'=8,'grp'=4] {'grp'}, dimensions={1}, use_global_device_ids=true | all-gather | bytes 81920 | tf_op jit(solution)/shard_map/all_gather | solution.py:70
  92.1 31.3 %all_gather.27 = bf16[512,512]{1,0:T(8,128)(2,1)S(1)} all-gather(bf16[64,512]{1,0:T(8,128)(2,1)S(1)} %all_gather.26), channel_id=1, replica_groups=mesh['sub'=8,'grp'=4] {'sub'}, dimensions={0}, use_global_device_ids=true | all-gather | bytes 589824 | tf_op jit(solution)/shard_map/all_gather | solution.py:73
  127.8 19.0 %psum.71 = f32[128]{0:T(128)S(1)} all-reduce(f32[128]{0:T(128)S(1)} %get-tuple-element.32), channel_id=1, replica_groups=mesh['sub'=8,'grp'=4] {'sub'}, use_global_device_ids=true, to_apply=%region_5.7 | all-reduce | flops 128 | bytes 1024 | tf_op jit(solution)/shard_map/psum | solution.py:154
  147.1 17.2 %psum.72 = f32[128]{0:T(128)S(1)} all-reduce(f32[128]{0:T(128)S(1)} %multiply_reduce_fusion.7), channel_id=1, replica_groups=mesh['sub'=8,'grp'=4] {'sub'}, use_global_device_ids=true, to_apply=%region_7.9 | all-reduce | flops 128 | bytes 1024 | tf_op jit(solution)/shard_map/psum | solution.py:85
  176.7 3.2 multiply_add_fusion.1
  192.8 5.3 %all_gather.28 = bf16[64,512]{1,0:T(8,128)(2,1)S(1)} all-gather(bf16[64,128]{1,0:T(8,128)(2,1)S(1)} %fusion.1), channel_id=1, replica_groups=mesh['sub'=8,'grp'=4] {'grp'}, dimensions={1}, use_global_device_ids=true | all-gather | bytes 81920 | tf_op jit(solution)/shard_map/all_gather | solution.py:70
  198.1 31.5 %all_gather.29 = bf16[512,512]{1,0:T(8,128)(2,1)S(1)} all-gather(bf16[64,512]{1,0:T(8,128)(2,1)S(1)} %all_gather.28), channel_id=1, replica_groups=mesh['sub'=8,'grp'=4] {'sub'}, dimensions={0}, use_global_device_ids=true | all-gather | bytes 589824 | tf_op jit(solution)/shard_map/all_gather | solution.py:73
  234.8 18.1 %psum.73 = f32[128]{0:T(128)S(1)} all-reduce(f32[128]{0:T(128)S(1)} %get-tuple-element.34), channel_id=1, replica_groups=mesh['sub'=8,'grp'=4] {'sub'}, use_global_device_ids=true, to_apply=%region_11.13 | all-reduce | flops 128 | bytes 1024 | tf_op jit(solution)/shard_map/psum | solution.py:154
  254.2 18.2 %psum.74 = f32[128]{0:T(128)S(1)} all-reduce(f32[128]{0:T(128)S(1)} %multiply_reduce_fusion.5), channel_id=1, replica_groups=mesh['sub'=8,'grp'=4] {'sub'}, use_global_device_ids=true, to_apply=%region_13.15 | all-reduce | flops 128 | bytes 1024 | tf_op jit(solution)/shard_map/psum | solution.py:154
  274.4 18.3 %psum.75 = f32[128]{0:T(128)S(1)} all-reduce(f32[128]{0:T(128)S(1)} %get-tuple-element.14), channel_id=1, replica_groups=mesh['sub'=8,'grp'=4] {'sub'}, use_global_device_ids=true, to_apply=%region_15.17 | all-reduce | flops 128 | bytes 1024 | tf_op jit(solution)/shard_map/psum | solution.py:85
  299.1 3.5 convolution_add_fusion.5
  303.9 3.7 collective-permute-start.13
  314.1 3.1 scatter_fusion.5
  320.5 5.3 %all_gather.30 = bf16[64,512]{1,0:T(8,128)(2,1)S(1)} all-gather(bf16[64,128]{1,0:T(8,128)(2,1)S(1)} %fusion.2), channel_id=1, replica_groups=mesh['sub'=8,'grp'=4] {'grp'}, dimensions={1}, use_global_device_ids=true | all-gather | bytes 81920 | tf_op jit(solution)/shard_map/all_gather | solution.py:70
  325.8 31.3 %all_gather.31 = bf16[512,512]{1,0:T(8,128)(2,1)S(1)} all-gather(bf16[64,512]{1,0:T(8,128)(2,1)S(1)} %all_gather.30), channel_id=1, replica_groups=mesh['sub'=8,'grp'=4] {'sub'}, dimensions={0}, use_global_device_ids=true | all-gather | bytes 589824 | tf_op jit(solution)/shard_map/all_gather | solution.py:73
  362.4 21.4 %psum.76 = f32[128]{0:T(128)S(1)} all-reduce(f32[128]{0:T(128)S(1)} %get-tuple-element.36), channel_id=1, replica_groups=mesh['sub'=8,'grp'=4] {'sub'}, use_global_device_ids=true, to_apply=%region_19.21 | all-reduce | flops 128 | bytes 1024 | tf_op jit(solution)/shard_map/psum | solution.py:154
  385.0 17.1 %psum.77 = f32[128]{0:T(128)S(1)} all-reduce(f32[128]{0:T(128)S(1)} %multiply_reduce_fusion.2), channel_id=1, replica_groups=mesh['sub'=8,'grp'=4] {'sub'}, use_global_device_ids=true, to_apply=%region_21.23 | all-reduce | flops 128 | bytes 1024 | tf_op jit(solution)/shard_map/psum | solution.py:154
  404.4 19.1 %psum.78 = f32[128]{0:T(128)S(1)} all-reduce(f32[128]{0:T(128)S(1)} %get-tuple-element.12), channel_id=1, replica_groups=mesh['sub'=8,'grp'=4] {'sub'}, use_global_device_ids=true, to_apply=%region_23.25 | all-reduce | flops 128 | bytes 1024 | tf_op jit(solution)/shard_map/psum | solution.py:154
  425.0 17.1 %psum.79 = f32[128]{0:T(128)S(1)} all-reduce(f32[128]{0:T(128)S(1)} %multiply_reduce_fusion), channel_id=1, replica_groups=mesh['sub'=8,'grp'=4] {'sub'}, use_global_device_ids=true, to_apply=%region_25.27 | all-reduce | flops 128 | bytes 1024 | tf_op jit(solution)/shard_map/psum | solution.py:85
  (214 shorter events, 86.7 us)
Async XLA Ops:
  0.0 45.6 %copy-start = (bf16[1024,1024]{1,0:T(8,128)(2,1)S(1)}, bf16[1024,1024]{1,0:T(8,128)(2,1)}, u32[]{:S(2)}) copy-start(bf16[1024,1024]{1,0:T(8,128)(2,1)} %param.16) | copy-start | bytes 6291460
  0.0 45.6 %copy-start.2 = (f32[128,1024]{1,0:T(8,128)S(1)}, f32[128,1024]{1,0:T(8,128)}, u32[]{:S(2)}) copy-start(f32[128,1024]{1,0:T(8,128)} %param.13) | copy-start | bytes 1572868
  41.1 6.9 %collective-permute-start.2 = (bf16[16,128]{1,0:T(8,128)(2,1)S(1)}, bf16[16,128]{1,0:T(8,128)(2,1)S(1)}, u32[]{:S(2)}, u32[]{:S(2)}) collective-permute-start(bf16[16,128]{1,0:T(8,128)(2,1)S(1)} %get-tuple-element.27), channel_id=1, source_target_pairs={{0,3},{1,2},{2,1},{3,0},{4,7},{5,6},{6,5},{7,4},{8,11},{9,10},{10,... | collective-permute-start | bytes 12296 | tf_op jit(solution)/shard_map/ppermute | solution.py:21
  41.1 6.9 %collective-permute-start.1 = (bf16[16,128]{1,0:T(8,128)(2,1)S(1)}, bf16[16,128]{1,0:T(8,128)(2,1)S(1)}, u32[]{:S(2)}, u32[]{:S(2)}) collective-permute-start(bf16[16,128]{1,0:T(8,128)(2,1)S(1)} %get-tuple-element.28), channel_id=1, source_target_pairs={{0,2},{1,3},{2,0},{3,1},{4,6},{5,7},{6,4},{7,5},{8,10},{9,11},{10,... | collective-permute-start | bytes 12296 | tf_op jit(solution)/shard_map/ppermute | solution.py:21
  42.7 5.3 %collective-permute-start = (bf16[16,128]{1,0:T(8,128)(2,1)S(1)}, bf16[16,128]{1,0:T(8,128)(2,1)S(1)}, u32[]{:S(2)}, u32[]{:S(2)}) collective-permute-start(bf16[16,128]{1,0:T(8,128)(2,1)S(1)} %get-tuple-element.29), channel_id=1, source_target_pairs={{0,1},{1,0},{2,3},{3,2},{4,5},{5,4},{6,7},{7,6},{8,9},{9,8},{10,11... | collective-permute-start | bytes 12296 | tf_op jit(solution)/shard_map/ppermute | solution.py:21
  72.5 9.4 %collective-permute-start.4 = (bf16[128,128]{0,1:T(8,128)(2,1)S(1)}, bf16[128,128]{0,1:T(8,128)(2,1)S(1)}, u32[]{:S(2)}, u32[]{:S(2)}) collective-permute-start(bf16[128,128]{0,1:T(8,128)(2,1)S(1)} %select_bitcast_fusion.4), channel_id=1, source_target_pairs={{0,4},{4,8},{8,12},{12,16},{16,20},{20,24},{24,28},{28,0},{1,5},{5... | collective-permute-start | bytes 98312 | tf_op jit(solution)/shard_map/ppermute | solution.py:32
  72.7 9.5 %collective-permute-start.3 = (bf16[128,128]{0,1:T(8,128)(2,1)S(1)}, bf16[128,128]{0,1:T(8,128)(2,1)S(1)}, u32[]{:S(2)}, u32[]{:S(2)}) collective-permute-start(bf16[128,128]{0,1:T(8,128)(2,1)S(1)} %select_bitcast_fusion.5), channel_id=1, source_target_pairs={{4,0},{8,4},{12,8},{16,12},{20,16},{24,20},{28,24},{0,28},{5,1},{9... | collective-permute-start | bytes 98312 | tf_op jit(solution)/shard_map/ppermute | solution.py:35
  123.6 3.8 collective-permute-start.7
  123.6 3.8 collective-permute-start.6
  125.2 2.2 collective-permute-start.5
  172.0 10.0 %collective-permute-start.9 = (bf16[128,128]{0,1:T(8,128)(2,1)S(1)}, bf16[128,128]{0,1:T(8,128)(2,1)S(1)}, u32[]{:S(2)}, u32[]{:S(2)}) collective-permute-start(bf16[128,128]{0,1:T(8,128)(2,1)S(1)} %select_bitcast_fusion.2), channel_id=1, source_target_pairs={{0,4},{4,8},{8,12},{12,16},{16,20},{20,24},{24,28},{28,0},{1,5},{5... | collective-permute-start | bytes 98312 | tf_op jit(solution)/shard_map/ppermute | solution.py:32
  173.9 8.4 %collective-permute-start.8 = (bf16[128,128]{0,1:T(8,128)(2,1)S(1)}, bf16[128,128]{0,1:T(8,128)(2,1)}, u32[]{:S(2)}, u32[]{:S(2)}) collective-permute-start(bf16[128,128]{0,1:T(8,128)(2,1)S(1)} %select_bitcast_fusion.3), channel_id=1, source_target_pairs={{4,0},{8,4},{12,8},{16,12},{20,16},{24,20},{28,24},{0,28},{5,1},{9... | collective-permute-start | bytes 98312 | tf_op jit(solution)/shard_map/ppermute | solution.py:35
  229.7 4.0 collective-permute-start.12
  229.7 4.0 collective-permute-start.11
  231.3 2.4 collective-permute-start.10
  302.7 7.0 %collective-permute-start.14 = (bf16[128,128]{0,1:T(8,128)(2,1)S(1)}, bf16[128,128]{0,1:T(8,128)(2,1)S(1)}, u32[]{:S(2)}, u32[]{:S(2)}) collective-permute-start(bf16[128,128]{0,1:T(8,128)(2,1)S(1)} %select_bitcast_fusion), channel_id=1, source_target_pairs={{0,4},{4,8},{8,12},{12,16},{16,20},{20,24},{24,28},{28,0},{1,5},{5... | collective-permute-start | bytes 98312 | tf_op jit(solution)/shard_map/ppermute | solution.py:32
  303.9 6.0 %collective-permute-start.13 = (bf16[128,128]{0,1:T(8,128)(2,1)S(1)}, bf16[128,128]{0,1:T(8,128)(2,1)}, u32[]{:S(2)}, u32[]{:S(2)}) collective-permute-start(bf16[128,128]{0,1:T(8,128)(2,1)S(1)} %select_bitcast_fusion.1), channel_id=1, source_target_pairs={{4,0},{8,4},{12,8},{16,12},{20,16},{24,20},{28,24},{0,28},{5,1},{9... | collective-permute-start | bytes 98312 | tf_op jit(solution)/shard_map/ppermute | solution.py:35
  357.2 4.0 collective-permute-start.17
  357.3 4.0 collective-permute-start.16
  358.8 2.4 collective-permute-start.15
  385.0 57.1 %copy-start.31 = (f32[128]{0:T(128)S(1)}, f32[128]{0:T(128)}, u32[]{:S(2)}) copy-start(f32[128]{0:T(128)} %copy-done.30) | copy-start | bytes 1540
  385.0 57.1 %copy-start.34 = (f32[128]{0:T(128)S(1)}, f32[128]{0:T(128)}, u32[]{:S(2)}) copy-start(f32[128]{0:T(128)} %copy-done.33) | copy-start | bytes 1540
  385.0 57.1 %copy-start.38 = (f32[128]{0:T(128)S(1)}, f32[128]{0:T(128)}, u32[]{:S(2)}) copy-start(f32[128]{0:T(128)} %copy-done.37) | copy-start | bytes 1540
  385.0 57.1 %copy-start.40 = (f32[128]{0:T(128)S(1)}, f32[128]{0:T(128)}, u32[]{:S(2)}) copy-start(f32[128]{0:T(128)} %copy-done.39) | copy-start | bytes 1540
  (35 other events, 626.5 us)
